TPU v7x, 32 devices: a whole 2x2x4 slice. The times are simulated.
32 devices in a mesh: row: 4 (over y, x), col: 8 (over z, core).
Axes of the slice: x: 2, y: 2, z: 4, core: 2. Of those that a mesh axis runs over, the one named last changes fastest.
Arguments:
- points: int32 [16, 3, 1024], P('row', None, 'col'), may hold values from 0 to 31
- ranks: int32 [16], replicated, may hold values from 64 to 256, as said below
- bases: bfloat16 [16, 1024, 256], P('row', 'col'), may hold values from -0.375 to 0.375
- pivots: bfloat16 [2, 256, 256], replicated, may hold values from -0.119628906 to 0.119628906
- probes: bfloat16 [16, 64, 1024], P('col'), may hold values from -0.119628906 to 0.119628906
Outputs:
- updated: bfloat16 [16, 16, 256, 256], P('row', 'col')
- images: float32 [16, 64, 1024], P('row', None, 'col')
Inputs may be any that keep to these rules, and one draw needn't show every extreme that they name: `ranks`: the rank of each tile; some tile has rank 256 and some rank 256 // 4.
All inputs are finite; a program needn't handle non-finite values.
Results may differ from a plain program's by a relative error of at most 0.004.
The roundings to bfloat16 on the way count: a program that leaves them out, or rounds other values in their place, can miss the bound.
Values may be sent and summed in bfloat16 or wider, within the bound.
A program may use at most 64 MiB of HBM per device.

v0:
```python
import jax
import jax.numpy as jnp
from jax import lax
from jax.sharding import PartitionSpec as P

B = 1024
R = 256
PANELS = 2
nugget = 0.25
decay_length = 4.0
wave_length = 3.0


def spread(x, axis, root):
    mine = lax.axis_index(axis) == root
    return lax.psum(jnp.where(mine, x, jnp.zeros_like(x)), axis)


def kernel_block(rows, cols):
    diff = rows[:, :, None] - cols[:, None, :]
    dist = jnp.sqrt(jnp.sum(diff * diff, axis=0) + nugget)
    return (jnp.exp(-dist / decay_length) * jnp.cos(dist / wave_length)).astype(jnp.bfloat16)


def body(points, ranks, bases, pivots, probes):
    row_count = bases.shape[0]
    col_count = probes.shape[0]
    row_index = lax.axis_index("row")
    col_index = lax.axis_index("col")
    row_bases, row_points = (
        lax.all_gather(bases, "col", axis=1, tiled=True),
        lax.all_gather(points.astype(jnp.bfloat16), "col", axis=2, tiled=True),
    )
    root = col_index * col_count // row_count
    offset = col_index * col_count - root * row_count
    picked_bases = lax.dynamic_slice_in_dim(row_bases, offset, col_count, 0)
    picked_points = lax.dynamic_slice_in_dim(row_points, offset, col_count, 0)
    col_bases, col_points = (spread(picked_bases, "row", root), spread(picked_points, "row", root))
    col_coords = col_points.astype(jnp.float32)
    block = min(B, 256)
    nblocks = B // block

    def row_tile(item):
        tile_points, tile_bases = item
        coords = tile_points.astype(jnp.float32).reshape(3, nblocks, block).transpose(1, 0, 2)
        basis_blocks = tile_bases.reshape(nblocks, block, R)

        def add_block(total, blk):
            block_points, block_bases = blk
            tiles = jax.vmap(lambda other: kernel_block(block_points, other))(col_coords)
            proj = jnp.einsum(
                "jnm,jmr->jnr", tiles, col_bases, preferred_element_type=jnp.float32
            ).astype(jnp.bfloat16)
            return (
                total
                + jnp.einsum("nr,jns->jrs", block_bases, proj, preferred_element_type=jnp.float32),
                None,
            )

        total, _ = lax.scan(
            add_block, jnp.zeros((col_count, R, R), jnp.float32), (coords, basis_blocks)
        )
        return total

    raw = lax.map(row_tile, (row_points, row_bases))
    rank_iota = jnp.arange(R, dtype=jnp.int32)
    row_ranks = lax.dynamic_slice_in_dim(ranks, row_index * row_count, row_count)
    col_ranks = lax.dynamic_slice_in_dim(ranks, col_index * col_count, col_count)
    row_mask = (rank_iota[None, :] < row_ranks[:, None]).astype(jnp.float32)
    col_mask = (rank_iota[None, :] < col_ranks[:, None]).astype(jnp.float32)
    cores = (raw * row_mask[:, None, :, None] * col_mask[None, :, None, :]).astype(jnp.bfloat16)
    row_panel = spread(cores, "col", 0)
    col_panel = spread(cores[:PANELS], "row", 0)
    left = jnp.einsum(
        "ikab,kbc->ikac", row_panel, pivots, preferred_element_type=jnp.float32
    ).astype(jnp.bfloat16)
    update = jnp.einsum("ikac,kjcd->ijad", left, col_panel, preferred_element_type=jnp.float32)
    row_ids = row_index * row_count + jnp.arange(row_count, dtype=jnp.int32)
    col_ids = col_index * col_count + jnp.arange(col_count, dtype=jnp.int32)
    trailing = (row_ids >= PANELS)[:, None] & (col_ids >= PANELS)[None, :]
    updated = (
        cores.astype(jnp.float32) - jnp.where(trailing[:, :, None, None], update, 0.0)
    ).astype(jnp.bfloat16)
    probe_cores = jnp.einsum(
        "jpn,jnr->jpr", probes, col_bases, preferred_element_type=jnp.float32
    ).astype(jnp.bfloat16)
    partial_cores = jnp.einsum(
        "ijab,jpb->ipa", updated, probe_cores, preferred_element_type=jnp.float32
    )
    summed = lax.psum(partial_cores, "col")
    images = jnp.einsum(
        "ipa,ina->ipn", summed, bases.astype(jnp.float32), precision=lax.Precision.HIGHEST
    )
    return (updated, images)


def solution(mesh):
    placed = (P("row", None, "col"), P(), P("row", "col", None), P(), P("col", None, None))
    return jax.shard_map(
        body,
        mesh=mesh,
        in_specs=placed,
        out_specs=(P("row", "col", None, None), P("row", None, "col")),
        check_vma=False,
    )
```

profile of v0, /device:TPU:0, one launch (start us, length us, event | category | flops | bytes accessed | tf_op | source)
XLA Modules:
  0.0 444.0 jit_solution(3983174135087618088)
XLA Ops:
  8.0 33.5 %all-gather.2.cloned.1.call-done = bf16[4,1024,256]{2,1,0:T(8,128)(2,1)} async-done(((bf16[4,128,256]{2,1,0:T(8,128)(2,1)}), bf16[4,1024,256]{2,1,0:T(8,128)(2,1)}) %all-gather.2.cloned.1.call-update) | async-done | bytes 2097168 | tf_op jit(solution)/shard_map/all_gather | solution.py:31
  43.9 10.4 %all_gather.6 = bf16[4,3,1024]{2,0,1:T(4,128)(2,1)S(1)} all-gather(bf16[4,3,128]{2,0,1:T(4,128)(2,1)S(1)} %convert_element_type.53), channel_id=1, replica_groups=mesh['row'=4,'col'=8] {'col'}, dimensions={2}, use_global_device_ids=true | all-gather | bytes 27648 | tf_op jit(solution)/shard_map/all_gather | solution.py:32
  54.3 16.0 %psum.35 = bf16[2,3,1024]{2,0,1:T(2,128)(2,1)S(1)} all-reduce(bf16[2,3,1024]{2,0,1:T(2,128)(2,1)S(1)} %broadcast_select_fusion.1), channel_id=1, replica_groups=mesh['row'=4,'col'=8] {'row'}, use_global_device_ids=true, to_apply=%region_0.1 | all-reduce | flops 6144 | bytes 24576 | tf_op jit(solution)/shard_map/psum | solution.py:16
  70.6 26.7 %all-reduce.5.cloned.1.call-done = bf16[2,1024,256]{2,1,0:T(8,128)(2,1)} async-done(((bf16[2,1024,256]{2,1,0:T(8,128)(2,1)}), bf16[2,1024,256]{2,1,0:T(8,128)(2,1)}) %all-reduce.5.cloned.1.call-update) | async-done | bytes 1048592 | tf_op jit(solution)/shard_map/psum | solution.py:16
  97.3 168.2 %while.25 = (s32[]{:T(128)}, f32[4,2,256,256]{3,2,1,0:T(8,128)}, bf16[4,3,1024]{2,1,0:T(4,128)(2,1)S(1)}, bf16[4,1024,256]{2,1,0:T(8,128)(2,1)}, f32[2,3,1024]{2...) while((s32[]{:T(128)}, f32[4,2,256,256]{3,2,1,0:T(8,128)}, ...), condition=%wide.region_6.7_spmd.clone, body=%wide.region_2.6_spmd.sunk.clone | while | flops 343280640 | bytes 9633548 | solution.py:65
  98.4 39.9 %while.24 = (s32[]{:T(128)}, f32[2,256,256]{1,2,0:T(8,128)S(1)}, f32[4,3,256]{2,1,0:T(4,128)S(1)}, f32[2,3,1024]{2,1,0:T(4,128)S(1)}, bf16[2,1024,256]{2,1,0:T(8...) while((s32[]{:T(128)}, f32[2,256,256]{1,2,0:T(8,128)S(1)}, ...), condition=%wide.region_5.5_spmd.clone, body=%wide.region_3.4_spmd.clone.sunk | while | flops 343277568 | bytes 6456423 | solution.py:60
  109.1 9.3 %fusion.31 = f32[2,256,256]{1,2,0:T(8,128)S(1)} fusion(bf16[2,1024,256]{2,1,0:T(8,128)(2,1)} %get-tuple-element.269, f32[2,256,1024]{2,1,0:T(8,128)S(1)} %multiply_reduce_fusion.2, f32[2,256,256]{1,2,0:T(8,128)S(1)} %get-tuple-element.258, pred[]{:T(512)S(6)} %compare.5, bf16[4,256,256]{2,1,0:T(8,128)(2,1)S(1)} %get-tuple-element.270, ...), kind=kOutput, calls=%fused_computation.3.clone.1 | convolution fusion | flops 339083264 | bytes 4325381 | tf_op jit(solution)/shard_map/while/body/eval_jaxpr/while/body/eval_jaxpr/nr,jns->jrs/dot_general | solution.py:56
  119.1 9.3 %fusion.31 = f32[2,256,256]{1,2,0:T(8,128)S(1)} fusion(bf16[2,1024,256]{2,1,0:T(8,128)(2,1)} %get-tuple-element.269, f32[2,256,1024]{2,1,0:T(8,128)S(1)} %multiply_reduce_fusion.2, f32[2,256,256]{1,2,0:T(8,128)S(1)} %get-tuple-element.258, pred[]{:T(512)S(6)} %compare.5, bf16[4,256,256]{2,1,0:T(8,128)(2,1)S(1)} %get-tuple-element.270, ...), kind=kOutput, calls=%fused_computation.3.clone.1 | convolution fusion | flops 339083264 | bytes 4325381 | tf_op jit(solution)/shard_map/while/body/eval_jaxpr/while/body/eval_jaxpr/nr,jns->jrs/dot_general | solution.py:56
  129.0 9.3 %fusion.31 = f32[2,256,256]{1,2,0:T(8,128)S(1)} fusion(bf16[2,1024,256]{2,1,0:T(8,128)(2,1)} %get-tuple-element.269, f32[2,256,1024]{2,1,0:T(8,128)S(1)} %multiply_reduce_fusion.2, f32[2,256,256]{1,2,0:T(8,128)S(1)} %get-tuple-element.258, pred[]{:T(512)S(6)} %compare.5, bf16[4,256,256]{2,1,0:T(8,128)(2,1)S(1)} %get-tuple-element.270, ...), kind=kOutput, calls=%fused_computation.3.clone.1 | convolution fusion | flops 339083264 | bytes 4325381 | tf_op jit(solution)/shard_map/while/body/eval_jaxpr/while/body/eval_jaxpr/nr,jns->jrs/dot_general | solution.py:56
  140.5 39.9 %while.24 = (s32[]{:T(128)}, f32[2,256,256]{1,2,0:T(8,128)S(1)}, f32[4,3,256]{2,1,0:T(4,128)S(1)}, f32[2,3,1024]{2,1,0:T(4,128)S(1)}, bf16[2,1024,256]{2,1,0:T(8...) while((s32[]{:T(128)}, f32[2,256,256]{1,2,0:T(8,128)S(1)}, ...), condition=%wide.region_5.5_spmd.clone, body=%wide.region_3.4_spmd.clone.sunk | while | flops 343277568 | bytes 6456423 | solution.py:60
  141.2 9.3 %fusion.31 = f32[2,256,256]{1,2,0:T(8,128)S(1)} fusion(bf16[2,1024,256]{2,1,0:T(8,128)(2,1)} %get-tuple-element.269, f32[2,256,1024]{2,1,0:T(8,128)S(1)} %multiply_reduce_fusion.2, f32[2,256,256]{1,2,0:T(8,128)S(1)} %get-tuple-element.258, pred[]{:T(512)S(6)} %compare.5, bf16[4,256,256]{2,1,0:T(8,128)(2,1)S(1)} %get-tuple-element.270, ...), kind=kOutput, calls=%fused_computation.3.clone.1 | convolution fusion | flops 339083264 | bytes 4325381 | tf_op jit(solution)/shard_map/while/body/eval_jaxpr/while/body/eval_jaxpr/nr,jns->jrs/dot_general | solution.py:56
  151.2 9.3 %fusion.31 = f32[2,256,256]{1,2,0:T(8,128)S(1)} fusion(bf16[2,1024,256]{2,1,0:T(8,128)(2,1)} %get-tuple-element.269, f32[2,256,1024]{2,1,0:T(8,128)S(1)} %multiply_reduce_fusion.2, f32[2,256,256]{1,2,0:T(8,128)S(1)} %get-tuple-element.258, pred[]{:T(512)S(6)} %compare.5, bf16[4,256,256]{2,1,0:T(8,128)(2,1)S(1)} %get-tuple-element.270, ...), kind=kOutput, calls=%fused_computation.3.clone.1 | convolution fusion | flops 339083264 | bytes 4325381 | tf_op jit(solution)/shard_map/while/body/eval_jaxpr/while/body/eval_jaxpr/nr,jns->jrs/dot_general | solution.py:56
  161.1 9.3 %fusion.31 = f32[2,256,256]{1,2,0:T(8,128)S(1)} fusion(bf16[2,1024,256]{2,1,0:T(8,128)(2,1)} %get-tuple-element.269, f32[2,256,1024]{2,1,0:T(8,128)S(1)} %multiply_reduce_fusion.2, f32[2,256,256]{1,2,0:T(8,128)S(1)} %get-tuple-element.258, pred[]{:T(512)S(6)} %compare.5, bf16[4,256,256]{2,1,0:T(8,128)(2,1)S(1)} %get-tuple-element.270, ...), kind=kOutput, calls=%fused_computation.3.clone.1 | convolution fusion | flops 339083264 | bytes 4325381 | tf_op jit(solution)/shard_map/while/body/eval_jaxpr/while/body/eval_jaxpr/nr,jns->jrs/dot_general | solution.py:56
  171.1 9.3 %fusion.31 = f32[2,256,256]{1,2,0:T(8,128)S(1)} fusion(bf16[2,1024,256]{2,1,0:T(8,128)(2,1)} %get-tuple-element.269, f32[2,256,1024]{2,1,0:T(8,128)S(1)} %multiply_reduce_fusion.2, f32[2,256,256]{1,2,0:T(8,128)S(1)} %get-tuple-element.258, pred[]{:T(512)S(6)} %compare.5, bf16[4,256,256]{2,1,0:T(8,128)(2,1)S(1)} %get-tuple-element.270, ...), kind=kOutput, calls=%fused_computation.3.clone.1 | convolution fusion | flops 339083264 | bytes 4325381 | tf_op jit(solution)/shard_map/while/body/eval_jaxpr/while/body/eval_jaxpr/nr,jns->jrs/dot_general | solution.py:56
  182.5 39.9 %while.24 = (s32[]{:T(128)}, f32[2,256,256]{1,2,0:T(8,128)S(1)}, f32[4,3,256]{2,1,0:T(4,128)S(1)}, f32[2,3,1024]{2,1,0:T(4,128)S(1)}, bf16[2,1024,256]{2,1,0:T(8...) while((s32[]{:T(128)}, f32[2,256,256]{1,2,0:T(8,128)S(1)}, ...), condition=%wide.region_5.5_spmd.clone, body=%wide.region_3.4_spmd.clone.sunk | while | flops 343277568 | bytes 6456423 | solution.py:60
  183.2 9.3 %fusion.31 = f32[2,256,256]{1,2,0:T(8,128)S(1)} fusion(bf16[2,1024,256]{2,1,0:T(8,128)(2,1)} %get-tuple-element.269, f32[2,256,1024]{2,1,0:T(8,128)S(1)} %multiply_reduce_fusion.2, f32[2,256,256]{1,2,0:T(8,128)S(1)} %get-tuple-element.258, pred[]{:T(512)S(6)} %compare.5, bf16[4,256,256]{2,1,0:T(8,128)(2,1)S(1)} %get-tuple-element.270, ...), kind=kOutput, calls=%fused_computation.3.clone.1 | convolution fusion | flops 339083264 | bytes 4325381 | tf_op jit(solution)/shard_map/while/body/eval_jaxpr/while/body/eval_jaxpr/nr,jns->jrs/dot_general | solution.py:56
  203.2 9.3 %fusion.31 = f32[2,256,256]{1,2,0:T(8,128)S(1)} fusion(bf16[2,1024,256]{2,1,0:T(8,128)(2,1)} %get-tuple-element.269, f32[2,256,1024]{2,1,0:T(8,128)S(1)} %multiply_reduce_fusion.2, f32[2,256,256]{1,2,0:T(8,128)S(1)} %get-tuple-element.258, pred[]{:T(512)S(6)} %compare.5, bf16[4,256,256]{2,1,0:T(8,128)(2,1)S(1)} %get-tuple-element.270, ...), kind=kOutput, calls=%fused_computation.3.clone.1 | convolution fusion | flops 339083264 | bytes 4325381 | tf_op jit(solution)/shard_map/while/body/eval_jaxpr/while/body/eval_jaxpr/nr,jns->jrs/dot_general | solution.py:56
  213.2 9.3 %fusion.31 = f32[2,256,256]{1,2,0:T(8,128)S(1)} fusion(bf16[2,1024,256]{2,1,0:T(8,128)(2,1)} %get-tuple-element.269, f32[2,256,1024]{2,1,0:T(8,128)S(1)} %multiply_reduce_fusion.2, f32[2,256,256]{1,2,0:T(8,128)S(1)} %get-tuple-element.258, pred[]{:T(512)S(6)} %compare.5, bf16[4,256,256]{2,1,0:T(8,128)(2,1)S(1)} %get-tuple-element.270, ...), kind=kOutput, calls=%fused_computation.3.clone.1 | convolution fusion | flops 339083264 | bytes 4325381 | tf_op jit(solution)/shard_map/while/body/eval_jaxpr/while/body/eval_jaxpr/nr,jns->jrs/dot_general | solution.py:56
  224.6 39.9 %while.24 = (s32[]{:T(128)}, f32[2,256,256]{1,2,0:T(8,128)S(1)}, f32[4,3,256]{2,1,0:T(4,128)S(1)}, f32[2,3,1024]{2,1,0:T(4,128)S(1)}, bf16[2,1024,256]{2,1,0:T(8...) while((s32[]{:T(128)}, f32[2,256,256]{1,2,0:T(8,128)S(1)}, ...), condition=%wide.region_5.5_spmd.clone, body=%wide.region_3.4_spmd.clone.sunk | while | flops 343277568 | bytes 6456423 | solution.py:60
  225.3 9.3 %fusion.31 = f32[2,256,256]{1,2,0:T(8,128)S(1)} fusion(bf16[2,1024,256]{2,1,0:T(8,128)(2,1)} %get-tuple-element.269, f32[2,256,1024]{2,1,0:T(8,128)S(1)} %multiply_reduce_fusion.2, f32[2,256,256]{1,2,0:T(8,128)S(1)} %get-tuple-element.258, pred[]{:T(512)S(6)} %compare.5, bf16[4,256,256]{2,1,0:T(8,128)(2,1)S(1)} %get-tuple-element.270, ...), kind=kOutput, calls=%fused_computation.3.clone.1 | convolution fusion | flops 339083264 | bytes 4325381 | tf_op jit(solution)/shard_map/while/body/eval_jaxpr/while/body/eval_jaxpr/nr,jns->jrs/dot_general | solution.py:56
  255.2 9.3 %fusion.31 = f32[2,256,256]{1,2,0:T(8,128)S(1)} fusion(bf16[2,1024,256]{2,1,0:T(8,128)(2,1)} %get-tuple-element.269, f32[2,256,1024]{2,1,0:T(8,128)S(1)} %multiply_reduce_fusion.2, f32[2,256,256]{1,2,0:T(8,128)S(1)} %get-tuple-element.258, pred[]{:T(512)S(6)} %compare.5, bf16[4,256,256]{2,1,0:T(8,128)(2,1)S(1)} %get-tuple-element.270, ...), kind=kOutput, calls=%fused_computation.3.clone.1 | convolution fusion | flops 339083264 | bytes 4325381 | tf_op jit(solution)/shard_map/while/body/eval_jaxpr/while/body/eval_jaxpr/nr,jns->jrs/dot_general | solution.py:56
  270.1 44.8 %all-reduce.7.cloned.1.call-done = bf16[2,2,256,256]{3,2,1,0:T(8,128)(2,1)} async-done(((bf16[2,2,256,256]{3,2,1,0:T(8,128)(2,1)}), bf16[2,2,256,256]{3,2,1,0:T(8,128)(2,1)}) %all-reduce.7.cloned.1.call-update) | async-done | bytes 524304 | tf_op jit(solution)/shard_map/psum | solution.py:16
  314.8 61.6 %all-reduce.9.cloned.1.call-done = bf16[4,2,256,256]{3,2,1,0:T(8,128)(2,1)} async-done(((bf16[4,2,256,256]{3,2,1,0:T(8,128)(2,1)}), bf16[4,2,256,256]{3,2,1,0:T(8,128)(2,1)}) %all-reduce.9.cloned.1.call-update) | async-done | bytes 1048592 | tf_op jit(solution)/shard_map/psum | solution.py:16
  381.5 54.0 %all-reduce.11.cloned.1.call-done = f32[4,64,256]{2,1,0:T(8,128)} async-done(((f32[4,64,256]{2,1,0:T(8,128)}), f32[4,64,256]{2,1,0:T(8,128)}) %all-reduce.11.cloned.1.call-update) | async-done | bytes 262160 | tf_op jit(solution)/shard_map/psum | solution.py:90
  (100 shorter events, 71.1 us)
Async XLA Ops:
  7.2 369.3 %copy-start = (bf16[2,256,256]{2,1,0:T(8,128)(2,1)S(1)}, bf16[2,256,256]{2,1,0:T(8,128)(2,1)}, u32[]{:S(2)}) copy-start(bf16[2,256,256]{2,1,0:T(8,128)(2,1)} %param.12) | copy-start | bytes 786436
  7.2 36.7 %copy-start.4 = (s32[4,3,128]{2,0,1:T(4,128)S(1)}, s32[4,3,128]{2,0,1:T(4,128)}, u32[]{:S(2)}) copy-start(s32[4,3,128]{2,0,1:T(4,128)} %param.9) | copy-start | bytes 18436
  7.2 63.1 %copy-start.5 = (s32[16]{0:T(128)S(1)}, s32[16]{0:T(128)}, u32[]{:S(2)}) copy-start(s32[16]{0:T(128)} %param.10) | copy-start | bytes 196
  7.2 34.3 %all-gather.2.cloned.1.call-start = ((), (), s32[]{:S(2)}) async-start(), calls=%async_computation | async-start | bytes 2359296 | tf_op jit(solution)/shard_map/all_gather | solution.py:31
  7.9 89.4 %all-reduce.5.cloned.1.call-start = ((), (), s32[]{:S(2)}) async-start(), calls=%async_computation.1 | async-start | bytes 2097152 | tf_op jit(solution)/shard_map/psum | solution.py:16
  43.8 271.1 %all-reduce.7.cloned.1.call-start = ((), (), s32[]{:S(2)}) async-start(), calls=%async_computation.2 | async-start | bytes 1048576 | tf_op jit(solution)/shard_map/psum | solution.py:16
  269.3 107.1 %all-reduce.9.cloned.1.call-start = ((), (), s32[]{:S(2)}) async-start(), calls=%async_computation.3 | async-start | bytes 2097152 | tf_op jit(solution)/shard_map/psum | solution.py:16
  269.9 165.6 %all-reduce.11.cloned.1.call-start = ((), (), s32[]{:S(2)}) async-start(), calls=%async_computation.4 | async-start | bytes 524288 | tf_op jit(solution)/shard_map/psum | solution.py:90
  270.1 108.8 %copy-start.1 = (bf16[2,1024,256]{2,1,0:T(8,128)(2,1)S(1)}, bf16[2,1024,256]{2,1,0:T(8,128)(2,1)}, u32[]{:S(2)}) copy-start(bf16[2,1024,256]{2,1,0:T(8,128)(2,1)} %get-tuple-element.313) | copy-start | bytes 3145732
  378.9 58.6 %copy-start.2 = (bf16[4,2,256,256]{3,2,1,0:T(8,128)(2,1)}, bf16[4,2,256,256]{3,2,1,0:T(8,128)(2,1)S(1)}, u32[]{:S(2)}) copy-start(bf16[4,2,256,256]{3,2,1,0:T(8,128)(2,1)S(1)} %fusion.11) | copy-start | bytes 3145732
  378.9 56.6 %copy-start.3 = (bf16[4,128,256]{2,1,0:T(8,128)(2,1)S(1)}, bf16[4,128,256]{2,1,0:T(8,128)(2,1)}, u32[]{:S(2)}) copy-start(bf16[4,128,256]{2,1,0:T(8,128)(2,1)} %param.11) | copy-start | bytes 786436
Sparse Core Ops, SparseCore 0:
  9.6 31.7 all-gather.1
  45.1 52.1 all-reduce.4
  269.5 45.3 all-reduce.6
  317.6 58.8 all-reduce.8
  381.6 53.8 all-reduce.10
where the time goes:
time: 445 us; the launch traced here: 444 us
  waiting for transfers between devices  222 us (50%)
  matrix products  155 us (35%)
  blocking collectives  26.4 us (6%)
  other arithmetic  16.8 us (4%)
  between operations  13.9 us (3%)
  local copies, waits for them, and re-layouts  8.84 us (2%)
    dot_general x16, matrix products, add_block(): jnp.einsum('nr,jns->jrs', block_bases, proj, preferred_element_type=jnp.f...  148 us
    psum x3, waiting for transfers between devices, spread(): return lax.psum(jnp.where(mine, x, jnp.zeros_like(x)), axis)  133 us
    psum x1, waiting for transfers between devices, body(): summed = lax.psum(partial_cores, 'col')  54 us
    all_gather x1, waiting for transfers between devices, body(): lax.all_gather(bases, 'col', axis=1, tiled=True)  33.5 us
    psum x1, blocking collectives, spread(): return lax.psum(jnp.where(mine, x, jnp.zeros_like(x)), axis)  16 us
    reduce_sum x16, other arithmetic, kernel_block(): dist = jnp.sqrt(jnp.sum(diff * diff, axis=0) + nugget)  10.5 us
    all_gather x1, blocking collectives, body(): lax.all_gather(points.astype(jnp.bfloat16), 'col', axis=2, tiled=True)  10.4 us
  transfers between devices with their start and end apart: 5, of which 5 were waited for; matrix products, arithmetic and copies ran while one was open for 0% of the time, Pallas kernels for 0%

commit v1 on v0

--- a/solution.py
+++ b/solution.py
@@ -87,7 +87,7 @@
     partial_cores = jnp.einsum(
         "ijab,jpb->ipa", updated, probe_cores, preferred_element_type=jnp.float32
     )
-    summed = lax.psum(partial_cores, "col")
+    summed = jnp.sum(lax.all_gather(partial_cores, "col"), axis=0)
     images = jnp.einsum(
         "ipa,ina->ipn", summed, bases.astype(jnp.float32), precision=lax.Precision.HIGHEST
     )

time: 445 us -> 420 us (0.944)
  waiting for transfers between devices: 222 us -> 196 us
    psum x1 -> x0, waiting for transfers between devices: 54 us -> none  [body(): summed = lax.psum(partial_cores, 'col')]
    all_gather x0 -> x1, waiting for transfers between devices: none -> 28.2 us  [body(): summed = jnp.sum(lax.all_gather(partial_cores, 'col'), axis=0)]
where the time goes in v1:
time: 420 us; the launch traced here: 419 us
  waiting for transfers between devices  196 us (47%)
  matrix products  154 us (37%)
  blocking collectives  26.4 us (6%)
  other arithmetic  18.6 us (4%)
  between operations  13.9 us (3%)
  local copies, waits for them, and re-layouts  8.84 us (2%)
    dot_general x16, matrix products, add_block(): jnp.einsum('nr,jns->jrs', block_bases, proj, preferred_element_type=jnp.f...  148 us
    psum x3, waiting for transfers between devices, spread(): return lax.psum(jnp.where(mine, x, jnp.zeros_like(x)), axis)  133 us
    all_gather x1, waiting for transfers between devices, body(): lax.all_gather(bases, 'col', axis=1, tiled=True)  33.5 us
    all_gather x1, waiting for transfers between devices, body(): summed = jnp.sum(lax.all_gather(partial_cores, 'col'), axis=0)  28.2 us
    psum x1, blocking collectives, spread(): return lax.psum(jnp.where(mine, x, jnp.zeros_like(x)), axis)  16 us
    reduce_sum x16, other arithmetic, kernel_block(): dist = jnp.sqrt(jnp.sum(diff * diff, axis=0) + nugget)  10.5 us
    all_gather x1, blocking collectives, body(): lax.all_gather(points.astype(jnp.bfloat16), 'col', axis=2, tiled=True)  10.4 us
  transfers between devices with their start and end apart: 5, of which 5 were waited for; matrix products, arithmetic and copies ran while one was open for 0% of the time, Pallas kernels for 0%

profile of v1, /device:TPU:0, one launch (start us, length us, event | category | flops | bytes accessed | tf_op | source)
XLA Modules:
  0.0 419.0 jit_solution(7669399850159658707)
XLA Ops:
  8.0 33.5 %all-gather.4.cloned.1.call-done = bf16[4,1024,256]{2,1,0:T(8,128)(2,1)} async-done(((bf16[4,128,256]{2,1,0:T(8,128)(2,1)}), bf16[4,1024,256]{2,1,0:T(8,128)(2,1)}) %all-gather.4.cloned.1.call-update) | async-done | bytes 2097168 | tf_op jit(solution)/shard_map/all_gather | solution.py:31
  43.9 10.4 %all_gather.12 = bf16[4,3,1024]{2,0,1:T(4,128)(2,1)S(1)} all-gather(bf16[4,3,128]{2,0,1:T(4,128)(2,1)S(1)} %convert_element_type.53), channel_id=1, replica_groups=mesh['row'=4,'col'=8] {'col'}, dimensions={2}, use_global_device_ids=true | all-gather | bytes 27648 | tf_op jit(solution)/shard_map/all_gather | solution.py:32
  54.3 16.0 %psum.28 = bf16[2,3,1024]{2,0,1:T(2,128)(2,1)S(1)} all-reduce(bf16[2,3,1024]{2,0,1:T(2,128)(2,1)S(1)} %broadcast_select_fusion.1), channel_id=1, replica_groups=mesh['row'=4,'col'=8] {'row'}, use_global_device_ids=true, to_apply=%region_0.1 | all-reduce | flops 6144 | bytes 24576 | tf_op jit(solution)/shard_map/psum | solution.py:16
  70.6 26.7 %all-reduce.4.cloned.1.call-done = bf16[2,1024,256]{2,1,0:T(8,128)(2,1)} async-done(((bf16[2,1024,256]{2,1,0:T(8,128)(2,1)}), bf16[2,1024,256]{2,1,0:T(8,128)(2,1)}) %all-reduce.4.cloned.1.call-update) | async-done | bytes 1048592 | tf_op jit(solution)/shard_map/psum | solution.py:16
  97.3 168.2 %while.25 = (s32[]{:T(128)}, f32[4,2,256,256]{3,2,1,0:T(8,128)}, bf16[4,3,1024]{2,1,0:T(4,128)(2,1)S(1)}, bf16[4,1024,256]{2,1,0:T(8,128)(2,1)}, f32[2,3,1024]{2...) while((s32[]{:T(128)}, f32[4,2,256,256]{3,2,1,0:T(8,128)}, ...), condition=%wide.region_6.7_spmd.clone, body=%wide.region_2.6_spmd.sunk.clone | while | flops 343280640 | bytes 9633548 | solution.py:65
  98.4 39.9 %while.24 = (s32[]{:T(128)}, f32[2,256,256]{1,2,0:T(8,128)S(1)}, f32[4,3,256]{2,1,0:T(4,128)S(1)}, f32[2,3,1024]{2,1,0:T(4,128)S(1)}, bf16[2,1024,256]{2,1,0:T(8...) while((s32[]{:T(128)}, f32[2,256,256]{1,2,0:T(8,128)S(1)}, ...), condition=%wide.region_5.5_spmd.clone, body=%wide.region_3.4_spmd.clone.sunk | while | flops 343277568 | bytes 6456423 | solution.py:60
  99.1 9.3 %fusion.31 = f32[2,256,256]{1,2,0:T(8,128)S(1)} fusion(bf16[2,1024,256]{2,1,0:T(8,128)(2,1)} %get-tuple-element.275, f32[2,256,1024]{2,1,0:T(8,128)S(1)} %multiply_reduce_fusion.2, f32[2,256,256]{1,2,0:T(8,128)S(1)} %get-tuple-element.264, pred[]{:T(512)S(6)} %compare.5, bf16[4,256,256]{2,1,0:T(8,128)(2,1)S(1)} %get-tuple-element.276, ...), kind=kOutput, calls=%fused_computation.3.clone.1 | convolution fusion | flops 339083264 | bytes 4325381 | tf_op jit(solution)/shard_map/while/body/eval_jaxpr/while/body/eval_jaxpr/nr,jns->jrs/dot_general | solution.py:56
  109.1 9.3 %fusion.31 = f32[2,256,256]{1,2,0:T(8,128)S(1)} fusion(bf16[2,1024,256]{2,1,0:T(8,128)(2,1)} %get-tuple-element.275, f32[2,256,1024]{2,1,0:T(8,128)S(1)} %multiply_reduce_fusion.2, f32[2,256,256]{1,2,0:T(8,128)S(1)} %get-tuple-element.264, pred[]{:T(512)S(6)} %compare.5, bf16[4,256,256]{2,1,0:T(8,128)(2,1)S(1)} %get-tuple-element.276, ...), kind=kOutput, calls=%fused_computation.3.clone.1 | convolution fusion | flops 339083264 | bytes 4325381 | tf_op jit(solution)/shard_map/while/body/eval_jaxpr/while/body/eval_jaxpr/nr,jns->jrs/dot_general | solution.py:56
  119.1 9.3 %fusion.31 = f32[2,256,256]{1,2,0:T(8,128)S(1)} fusion(bf16[2,1024,256]{2,1,0:T(8,128)(2,1)} %get-tuple-element.275, f32[2,256,1024]{2,1,0:T(8,128)S(1)} %multiply_reduce_fusion.2, f32[2,256,256]{1,2,0:T(8,128)S(1)} %get-tuple-element.264, pred[]{:T(512)S(6)} %compare.5, bf16[4,256,256]{2,1,0:T(8,128)(2,1)S(1)} %get-tuple-element.276, ...), kind=kOutput, calls=%fused_computation.3.clone.1 | convolution fusion | flops 339083264 | bytes 4325381 | tf_op jit(solution)/shard_map/while/body/eval_jaxpr/while/body/eval_jaxpr/nr,jns->jrs/dot_general | solution.py:56
  129.1 9.3 %fusion.31 = f32[2,256,256]{1,2,0:T(8,128)S(1)} fusion(bf16[2,1024,256]{2,1,0:T(8,128)(2,1)} %get-tuple-element.275, f32[2,256,1024]{2,1,0:T(8,128)S(1)} %multiply_reduce_fusion.2, f32[2,256,256]{1,2,0:T(8,128)S(1)} %get-tuple-element.264, pred[]{:T(512)S(6)} %compare.5, bf16[4,256,256]{2,1,0:T(8,128)(2,1)S(1)} %get-tuple-element.276, ...), kind=kOutput, calls=%fused_computation.3.clone.1 | convolution fusion | flops 339083264 | bytes 4325381 | tf_op jit(solution)/shard_map/while/body/eval_jaxpr/while/body/eval_jaxpr/nr,jns->jrs/dot_general | solution.py:56
  140.5 39.9 %while.24 = (s32[]{:T(128)}, f32[2,256,256]{1,2,0:T(8,128)S(1)}, f32[4,3,256]{2,1,0:T(4,128)S(1)}, f32[2,3,1024]{2,1,0:T(4,128)S(1)}, bf16[2,1024,256]{2,1,0:T(8...) while((s32[]{:T(128)}, f32[2,256,256]{1,2,0:T(8,128)S(1)}, ...), condition=%wide.region_5.5_spmd.clone, body=%wide.region_3.4_spmd.clone.sunk | while | flops 343277568 | bytes 6456423 | solution.py:60
  141.2 9.3 %fusion.31 = f32[2,256,256]{1,2,0:T(8,128)S(1)} fusion(bf16[2,1024,256]{2,1,0:T(8,128)(2,1)} %get-tuple-element.275, f32[2,256,1024]{2,1,0:T(8,128)S(1)} %multiply_reduce_fusion.2, f32[2,256,256]{1,2,0:T(8,128)S(1)} %get-tuple-element.264, pred[]{:T(512)S(6)} %compare.5, bf16[4,256,256]{2,1,0:T(8,128)(2,1)S(1)} %get-tuple-element.276, ...), kind=kOutput, calls=%fused_computation.3.clone.1 | convolution fusion | flops 339083264 | bytes 4325381 | tf_op jit(solution)/shard_map/while/body/eval_jaxpr/while/body/eval_jaxpr/nr,jns->jrs/dot_general | solution.py:56
  151.2 9.3 %fusion.31 = f32[2,256,256]{1,2,0:T(8,128)S(1)} fusion(bf16[2,1024,256]{2,1,0:T(8,128)(2,1)} %get-tuple-element.275, f32[2,256,1024]{2,1,0:T(8,128)S(1)} %multiply_reduce_fusion.2, f32[2,256,256]{1,2,0:T(8,128)S(1)} %get-tuple-element.264, pred[]{:T(512)S(6)} %compare.5, bf16[4,256,256]{2,1,0:T(8,128)(2,1)S(1)} %get-tuple-element.276, ...), kind=kOutput, calls=%fused_computation.3.clone.1 | convolution fusion | flops 339083264 | bytes 4325381 | tf_op jit(solution)/shard_map/while/body/eval_jaxpr/while/body/eval_jaxpr/nr,jns->jrs/dot_general | solution.py:56
  161.1 9.3 %fusion.31 = f32[2,256,256]{1,2,0:T(8,128)S(1)} fusion(bf16[2,1024,256]{2,1,0:T(8,128)(2,1)} %get-tuple-element.275, f32[2,256,1024]{2,1,0:T(8,128)S(1)} %multiply_reduce_fusion.2, f32[2,256,256]{1,2,0:T(8,128)S(1)} %get-tuple-element.264, pred[]{:T(512)S(6)} %compare.5, bf16[4,256,256]{2,1,0:T(8,128)(2,1)S(1)} %get-tuple-element.276, ...), kind=kOutput, calls=%fused_computation.3.clone.1 | convolution fusion | flops 339083264 | bytes 4325381 | tf_op jit(solution)/shard_map/while/body/eval_jaxpr/while/body/eval_jaxpr/nr,jns->jrs/dot_general | solution.py:56
  171.1 9.3 %fusion.31 = f32[2,256,256]{1,2,0:T(8,128)S(1)} fusion(bf16[2,1024,256]{2,1,0:T(8,128)(2,1)} %get-tuple-element.275, f32[2,256,1024]{2,1,0:T(8,128)S(1)} %multiply_reduce_fusion.2, f32[2,256,256]{1,2,0:T(8,128)S(1)} %get-tuple-element.264, pred[]{:T(512)S(6)} %compare.5, bf16[4,256,256]{2,1,0:T(8,128)(2,1)S(1)} %get-tuple-element.276, ...), kind=kOutput, calls=%fused_computation.3.clone.1 | convolution fusion | flops 339083264 | bytes 4325381 | tf_op jit(solution)/shard_map/while/body/eval_jaxpr/while/body/eval_jaxpr/nr,jns->jrs/dot_general | solution.py:56
  182.6 39.9 %while.24 = (s32[]{:T(128)}, f32[2,256,256]{1,2,0:T(8,128)S(1)}, f32[4,3,256]{2,1,0:T(4,128)S(1)}, f32[2,3,1024]{2,1,0:T(4,128)S(1)}, bf16[2,1024,256]{2,1,0:T(8...) while((s32[]{:T(128)}, f32[2,256,256]{1,2,0:T(8,128)S(1)}, ...), condition=%wide.region_5.5_spmd.clone, body=%wide.region_3.4_spmd.clone.sunk | while | flops 343277568 | bytes 6456423 | solution.py:60
  193.2 9.3 %fusion.31 = f32[2,256,256]{1,2,0:T(8,128)S(1)} fusion(bf16[2,1024,256]{2,1,0:T(8,128)(2,1)} %get-tuple-element.275, f32[2,256,1024]{2,1,0:T(8,128)S(1)} %multiply_reduce_fusion.2, f32[2,256,256]{1,2,0:T(8,128)S(1)} %get-tuple-element.264, pred[]{:T(512)S(6)} %compare.5, bf16[4,256,256]{2,1,0:T(8,128)(2,1)S(1)} %get-tuple-element.276, ...), kind=kOutput, calls=%fused_computation.3.clone.1 | convolution fusion | flops 339083264 | bytes 4325381 | tf_op jit(solution)/shard_map/while/body/eval_jaxpr/while/body/eval_jaxpr/nr,jns->jrs/dot_general | solution.py:56
  203.2 9.3 %fusion.31 = f32[2,256,256]{1,2,0:T(8,128)S(1)} fusion(bf16[2,1024,256]{2,1,0:T(8,128)(2,1)} %get-tuple-element.275, f32[2,256,1024]{2,1,0:T(8,128)S(1)} %multiply_reduce_fusion.2, f32[2,256,256]{1,2,0:T(8,128)S(1)} %get-tuple-element.264, pred[]{:T(512)S(6)} %compare.5, bf16[4,256,256]{2,1,0:T(8,128)(2,1)S(1)} %get-tuple-element.276, ...), kind=kOutput, calls=%fused_computation.3.clone.1 | convolution fusion | flops 339083264 | bytes 4325381 | tf_op jit(solution)/shard_map/while/body/eval_jaxpr/while/body/eval_jaxpr/nr,jns->jrs/dot_general | solution.py:56
  224.6 39.9 %while.24 = (s32[]{:T(128)}, f32[2,256,256]{1,2,0:T(8,128)S(1)}, f32[4,3,256]{2,1,0:T(4,128)S(1)}, f32[2,3,1024]{2,1,0:T(4,128)S(1)}, bf16[2,1024,256]{2,1,0:T(8...) while((s32[]{:T(128)}, f32[2,256,256]{1,2,0:T(8,128)S(1)}, ...), condition=%wide.region_5.5_spmd.clone, body=%wide.region_3.4_spmd.clone.sunk | while | flops 343277568 | bytes 6456423 | solution.py:60
  245.3 9.3 %fusion.31 = f32[2,256,256]{1,2,0:T(8,128)S(1)} fusion(bf16[2,1024,256]{2,1,0:T(8,128)(2,1)} %get-tuple-element.275, f32[2,256,1024]{2,1,0:T(8,128)S(1)} %multiply_reduce_fusion.2, f32[2,256,256]{1,2,0:T(8,128)S(1)} %get-tuple-element.264, pred[]{:T(512)S(6)} %compare.5, bf16[4,256,256]{2,1,0:T(8,128)(2,1)S(1)} %get-tuple-element.276, ...), kind=kOutput, calls=%fused_computation.3.clone.1 | convolution fusion | flops 339083264 | bytes 4325381 | tf_op jit(solution)/shard_map/while/body/eval_jaxpr/while/body/eval_jaxpr/nr,jns->jrs/dot_general | solution.py:56
  255.2 9.3 %fusion.31 = f32[2,256,256]{1,2,0:T(8,128)S(1)} fusion(bf16[2,1024,256]{2,1,0:T(8,128)(2,1)} %get-tuple-element.275, f32[2,256,1024]{2,1,0:T(8,128)S(1)} %multiply_reduce_fusion.2, f32[2,256,256]{1,2,0:T(8,128)S(1)} %get-tuple-element.264, pred[]{:T(512)S(6)} %compare.5, bf16[4,256,256]{2,1,0:T(8,128)(2,1)S(1)} %get-tuple-element.276, ...), kind=kOutput, calls=%fused_computation.3.clone.1 | convolution fusion | flops 339083264 | bytes 4325381 | tf_op jit(solution)/shard_map/while/body/eval_jaxpr/while/body/eval_jaxpr/nr,jns->jrs/dot_general | solution.py:56
  270.1 44.8 %all-reduce.6.cloned.1.call-done = bf16[2,2,256,256]{3,2,1,0:T(8,128)(2,1)} async-done(((bf16[2,2,256,256]{3,2,1,0:T(8,128)(2,1)}), bf16[2,2,256,256]{3,2,1,0:T(8,128)(2,1)}) %all-reduce.6.cloned.1.call-update) | async-done | bytes 524304 | tf_op jit(solution)/shard_map/psum | solution.py:16
  314.8 61.6 %all-reduce.8.cloned.1.call-done = bf16[4,2,256,256]{3,2,1,0:T(8,128)(2,1)} async-done(((bf16[4,2,256,256]{3,2,1,0:T(8,128)(2,1)}), bf16[4,2,256,256]{3,2,1,0:T(8,128)(2,1)}) %all-reduce.8.cloned.1.call-update) | async-done | bytes 1048592 | tf_op jit(solution)/shard_map/psum | solution.py:16
  381.5 28.2 %all-gather.6.cloned.1.call-done = f32[32,64,256]{2,1,0:T(8,128)} async-done(((f32[4,64,256]{2,1,0:T(8,128)}), f32[32,64,256]{2,1,0:T(8,128)}) %all-gather.6.cloned.1.call-update) | async-done | bytes 2097168 | tf_op jit(solution)/shard_map/all_gather | solution.py:90
  (101 shorter events, 71.9 us)
Async XLA Ops:
  7.2 369.3 %copy-start = (bf16[2,256,256]{2,1,0:T(8,128)(2,1)S(1)}, bf16[2,256,256]{2,1,0:T(8,128)(2,1)}, u32[]{:S(2)}) copy-start(bf16[2,256,256]{2,1,0:T(8,128)(2,1)} %param.12) | copy-start | bytes 786436
  7.2 36.7 %copy-start.4 = (s32[4,3,128]{2,0,1:T(4,128)S(1)}, s32[4,3,128]{2,0,1:T(4,128)}, u32[]{:S(2)}) copy-start(s32[4,3,128]{2,0,1:T(4,128)} %param.9) | copy-start | bytes 18436
  7.2 63.1 %copy-start.5 = (s32[16]{0:T(128)S(1)}, s32[16]{0:T(128)}, u32[]{:S(2)}) copy-start(s32[16]{0:T(128)} %param.10) | copy-start | bytes 196
  7.2 34.3 %all-gather.4.cloned.1.call-start = ((), (), s32[]{:S(2)}) async-start(), calls=%async_computation | async-start | bytes 2359296 | tf_op jit(solution)/shard_map/all_gather | solution.py:31
  7.9 89.4 %all-reduce.4.cloned.1.call-start = ((), (), s32[]{:S(2)}) async-start(), calls=%async_computation.1 | async-start | bytes 2097152 | tf_op jit(solution)/shard_map/psum | solution.py:16
  43.8 271.1 %all-reduce.6.cloned.1.call-start = ((), (), s32[]{:S(2)}) async-start(), calls=%async_computation.2 | async-start | bytes 1048576 | tf_op jit(solution)/shard_map/psum | solution.py:16
  269.4 107.1 %all-reduce.8.cloned.1.call-start = ((), (), s32[]{:S(2)}) async-start(), calls=%async_computation.3 | async-start | bytes 2097152 | tf_op jit(solution)/shard_map/psum | solution.py:16
  269.9 139.8 %all-gather.6.cloned.1.call-start = ((), (), s32[]{:S(2)}) async-start(), calls=%async_computation.4 | async-start | bytes 2359296 | tf_op jit(solution)/shard_map/all_gather | solution.py:90
  270.1 108.8 %copy-start.1 = (bf16[2,1024,256]{2,1,0:T(8,128)(2,1)S(1)}, bf16[2,1024,256]{2,1,0:T(8,128)(2,1)}, u32[]{:S(2)}) copy-start(bf16[2,1024,256]{2,1,0:T(8,128)(2,1)} %get-tuple-element.320) | copy-start | bytes 3145732
  378.9 32.6 %copy-start.2 = (bf16[4,2,256,256]{3,2,1,0:T(8,128)(2,1)}, bf16[4,2,256,256]{3,2,1,0:T(8,128)(2,1)S(1)}, u32[]{:S(2)}) copy-start(bf16[4,2,256,256]{3,2,1,0:T(8,128)(2,1)S(1)} %fusion.11) | copy-start | bytes 3145732
  378.9 32.6 %copy-start.3 = (bf16[4,128,256]{2,1,0:T(8,128)(2,1)S(1)}, bf16[4,128,256]{2,1,0:T(8,128)(2,1)}, u32[]{:S(2)}) copy-start(bf16[4,128,256]{2,1,0:T(8,128)(2,1)} %param.11) | copy-start | bytes 786436
Sparse Core Ops, SparseCore 0:
  9.6 31.7 all-gather.3
  45.1 52.1 all-reduce.3
  269.5 45.3 all-reduce.5
  317.6 58.8 all-reduce.7
  381.6 28.0 all-gather.5
